TPU v7x, 32 devices: a whole 2x2x4 slice. The times are simulated.
32 devices in a mesh: row: 8 (over y, x, core), col: 4 (over z).
Axes of the slice: x: 2, y: 2, z: 4, core: 2. Of those that a mesh axis runs over, the one named last changes fastest.
Arguments:
- record: bfloat16 [6, 2048, 2560], P(None, ('row', 'col')), may hold values from -6 to 6
- taps: float32 [200], replicated, may hold values from -0.4375 to 0.4375
- plan: int32 [6], replicated, may hold values from 0 to 5, each once
- quality: int32 [2048], P(('row', 'col')), may hold values 0 or 1
Outputs:
- correlation: float32 [51, 2048, 2048], P(None, 'row', 'col')
Inputs may be any that keep to these rules, and one draw needn't show every extreme that they name: plan is a permutation of the recorded sub-windows; its first 4 entries name the ones that are stacked.
All inputs are finite; a program needn't handle non-finite values. No bound on the sum of `quality` on one device may be relied on, other than what follows from the above.
Results may differ from a plain program's by a relative error of at most 0.0039.
Values may be sent and summed in bfloat16 or wider, within the bound.
A program may use at most 128 MiB of HBM per device.

v0:
```python
import functools
import math

import jax
import jax.numpy as jnp
from jax import lax
from jax.experimental import pallas as pl
from jax.experimental.pallas import tpu as pltpu
from jax.sharding import PartitionSpec as P

STRIDE = 20
TAPS = 200
HALFWIN = 32
MAXLAG = 25
SUB = 4
LAGS = 51
LANES = 128
BAND_FRAMES = 32
BAND_STEP = BAND_FRAMES * STRIDE
BAND_WIDTH = 896
PARTS = 3
LAG_GROUP = 3
SLOTS = 3
CHUNKS = 2

MESH = pl.DeviceIdType.MESH
NT = (((1,), (1,)), ((), ()))


def split_parts(values, count):
    parts = []
    for _ in range(count):
        part = values.astype(jnp.bfloat16)
        parts.append(part)
        values = values - part.astype(jnp.float32)
    return parts


def filter_band(tap_row):
    base = jnp.broadcast_to(tap_row, (8, TAPS))
    base = jnp.concatenate([base, jnp.zeros((8, BAND_WIDTH - TAPS), jnp.float32)], axis=1)
    place = lax.broadcasted_iota(jnp.int32, (8, BAND_WIDTH), 0)
    groups = []
    for group in range(BAND_FRAMES // 8):
        held = jnp.zeros((8, BAND_WIDTH), jnp.float32)
        for row in range(8):
            shift = (group * 8 + row) * STRIDE
            moved = base if shift == 0 else pltpu.roll(base, shift, 1)
            held = jnp.where(place == row, moved, held)
        groups.append(held)
    return jnp.concatenate(groups, axis=0)


def nearest_first(cols):
    return [sorted(range(cols), key=lambda other: (abs(other - c), other)) for c in range(cols)]


def whiten_and_send(
    rows, cols, plan_hbm, tap_hbm, quality_hbm, record_ref,
    source_ref, turned_ref,
    receiver_ref, raw, table, plan_ref, tap_ref, quality_ref,
    load_sem, keep_sem, source_sem, receiver_sem, out_sem, plane_sem, twin_sem,
):
    r, c = lax.axis_index("row"), lax.axis_index("col")
    parity = lax.rem(r, 2)
    pair = lax.div(r, 2)
    twin = r + 1 - 2 * parity
    on_diagonal = pair == c
    slots, chans, length = raw.shape
    frames = length // STRIDE
    bits = cols.bit_length() - 1

    loads = [
        pltpu.make_async_copy(tap_hbm, tap_ref, load_sem.at[slots]),
        pltpu.make_async_copy(plan_hbm, plan_ref, load_sem.at[slots + 1]),
        pltpu.make_async_copy(quality_hbm, quality_ref, load_sem.at[slots + 2]),
    ] + [pltpu.make_async_copy(record_ref.at[i], raw.at[i], load_sem.at[i]) for i in range(slots)]
    for load in loads:
        load.start()

    def bit(value, k):
        return lax.rem(lax.div(value, 2**k), 2)

    def across(k):
        return r + 2 * 2**k * (1 - 2 * bit(pair, k))

    def other_core(row):
        return row + 1 - 2 * parity

    barrier = pltpu.get_barrier_semaphore()

    def greet(row, col):
        pl.semaphore_signal(barrier, inc=1, device_id=(row, col), device_id_type=MESH)

    for step in range(1, cols):
        greet(r, lax.rem(c + step, cols))
    for k in range(bits):
        greet(across(k), c)
        greet(other_core(across(k)), c)
    greet(twin, c)

    table[...] = jnp.zeros_like(table)
    loads[0].wait()
    band = filter_band(tap_ref[...])
    for number, part in enumerate(split_parts(band, PARTS)):
        for block in range(frames // BAND_FRAMES):
            start = block * BAND_STEP
            width = min(BAND_WIDTH, length - start)
            first = number * frames + block * BAND_FRAMES
            table[first : first + BAND_FRAMES, start : start + width] = part[:, :width]

    for load in loads[1:]:
        load.wait()
    picked = jnp.concatenate([raw[plan_ref[s]] for s in range(SUB)], axis=0)
    summed = lax.dot_general(table[...], picked, NT, preferred_element_type=jnp.float32)
    decimated = summed[:frames]
    for number in range(1, PARTS):
        decimated = decimated + summed[number * frames : (number + 1) * frames]

    near = lax.broadcasted_iota(jnp.int32, (frames, frames), 0)
    near = jnp.abs(near - lax.broadcasted_iota(jnp.int32, (frames, frames), 1)) <= HALFWIN
    near = near.astype(jnp.float32).astype(jnp.bfloat16)
    windows = SUB // CHUNKS
    usable = jnp.concatenate([quality_ref[...].astype(jnp.float32)] * windows, axis=1)

    def whiten(chunk):
        part = decimated[:, chunk * windows * chans : (chunk + 1) * windows * chans]
        envelope = jnp.zeros_like(part)
        for piece in split_parts(jnp.abs(part), PARTS):
            envelope = envelope + jnp.dot(near, piece, preferred_element_type=jnp.float32)
        scaled = (part / (envelope / (2 * HALFWIN + 1) + 1e-05) * usable).T
        for s in range(windows):
            window = scaled[s * chans : (s + 1) * chans]
            source_ref[chunk, c, :, s * frames : (s + 1) * frames] = window.astype(jnp.bfloat16)

    def remote(src, dst, send_sem, recv_sem, row, col):
        return pltpu.make_async_remote_copy(
            src_ref=src, dst_ref=dst, send_sem=send_sem, recv_sem=recv_sem,
            device_id=(row, col), device_id_type=MESH,
        )

    def along(chunk, step):
        target = lax.rem(pair + step, cols)
        mine = source_ref.at[chunk, c]
        copy = remote(mine, mine, out_sem.at[chunk, step], source_sem.at[chunk, c], r, target)
        return target != c, copy

    def source_arrival(chunk, number):
        block = source_ref.at[chunk, number]
        return remote(
            block, block, out_sem.at[0, 0], source_sem.at[chunk, number],
            r, lax.rem(c + 1, cols),
        )

    half = parity * cols

    def receiver_arrival(chunk, number):
        block = receiver_ref.at[chunk, number]
        return remote(
            block, block, out_sem.at[0, 0], receiver_sem.at[chunk, number], twin, c
        )

    def hand_on(block, chunk, number, to, send_sem):
        return remote(
            block, receiver_ref.at[chunk, half + number], send_sem,
            receiver_sem.at[chunk, half + number], to, c,
        )

    for chunk in range(CHUNKS):
        whiten(chunk)
        if chunk == 0:
            pl.semaphore_wait(barrier, cols - 1 + 2 * bits + 1)
        other, copy = along(chunk, 0)
        pl.when(other)(copy.start)
    for chunk in range(CHUNKS):
        for step in range(1, cols):
            other, copy = along(chunk, step)
            pl.when(other)(copy.start)

    order = nearest_first(cols)

    def place(step):
        number = jnp.int32(order[0][step])
        for column in range(1, cols):
            number = jnp.where(c == column, order[column][step], number)
        return number

    differs = [bit(pair, k) != bit(c, k) for k in range(bits)]
    far = sum(jnp.where(differ, 1, 0) for differ in differs) > 1

    def passes_on(step, k):
        ahead = range(k + 1) if step % 2 == 0 else range(k, bits)
        free = jnp.logical_not(differs[k])
        for other in ahead:
            free = jnp.logical_and(free, jnp.logical_not(differs[other]))
        return free

    def kept(chunk, step):
        number = place(step)
        return pltpu.make_async_copy(
            source_ref.at[chunk, number],
            receiver_ref.at[chunk, half + number],
            keep_sem.at[chunk, step],
        )

    every = [(chunk, step) for chunk in range(CHUNKS) for step in range(cols)]

    @pl.when(on_diagonal)
    def _():
        for chunk, step in every:
            number = place(step)
            if step > 0:
                source_arrival(chunk, number).wait_recv()
            mine = source_ref.at[chunk, number]
            for k in range(bits):
                hand_on(mine, chunk, number, across(k), plane_sem.at[chunk, step, k, 0]).start()
            hand_on(mine, chunk, number, twin, twin_sem.at[chunk, step]).start()
            kept(chunk, step).start()
        for chunk, step in every:
            kept(chunk, step).wait()

    @pl.when(jnp.logical_not(on_diagonal))
    def _():
        for chunk, step in every:
            number = place(step)
            mine = receiver_ref.at[chunk, half + number]
            receiver_arrival(chunk, half + number).wait_recv()
            for k in range(bits):
                sends = passes_on(step, k)
                for core, to in enumerate((across(k), other_core(across(k)))):
                    pl.when(sends)(
                        hand_on(mine, chunk, number, to, plane_sem.at[chunk, step, k, core]).start
                    )
            pl.when(jnp.logical_not(far))(
                hand_on(mine, chunk, number, twin, twin_sem.at[chunk, step]).start
            )
        for chunk, step in every:
            if step > 0:
                source_arrival(chunk, lax.rem(c + step, cols)).wait_recv()

    width = windows * frames
    for chunk in range(CHUNKS):
        for number in range(cols):
            receiver_arrival(chunk, cols - half + number).wait_recv()
        whole = receiver_ref[chunk].reshape(2 * cols * chans, width)
        turned_ref[chunk * width : (chunk + 1) * width, :] = (
            whole.astype(jnp.float32).T.astype(jnp.bfloat16)
        )
    for chunk, step in every:
        other, copy = along(chunk, step)
        pl.when(other)(copy.wait_send)
        block = receiver_ref.at[chunk, half + step]
        for k in range(bits):
            sends = passes_on(step, k)
            pl.when(jnp.logical_or(on_diagonal, sends))(
                hand_on(block, chunk, step, across(k), plane_sem.at[chunk, step, k, 0]).wait_send
            )
            pl.when(jnp.logical_and(jnp.logical_not(on_diagonal), sends))(
                hand_on(block, chunk, step, across(k), plane_sem.at[chunk, step, k, 1]).wait_send
            )
        pl.when(jnp.logical_not(far))(
            hand_on(block, chunk, step, twin, twin_sem.at[chunk, step]).wait_send
        )


def correlate(scale, source_ref, turned, out_ref, even, odd, held, sems):
    frames = LANES
    chunks, sources, width = source_ref.shape
    windows = width // frames
    groups = out_ref.shape[0] // LAG_GROUP
    lane = lax.broadcasted_iota(jnp.int32, (sources, frames), 1)

    def send(group):
        slot = lax.rem(group, SLOTS)
        return pltpu.make_async_copy(
            held.at[slot], out_ref.at[pl.ds(group * LAG_GROUP, LAG_GROUP)], sems.at[slot]
        )

    def fill(moved, group, inner):
        lag = group * LAG_GROUP + inner - MAXLAG
        from_place = lane - lag
        inside = jnp.logical_and(from_place >= 0, from_place < frames)
        shift = lax.rem(lag + frames, frames)
        rows = slice(inner * sources, (inner + 1) * sources)
        for s in range(chunks * windows):
            place = s % windows * frames
            window = pltpu.roll(source_ref[s // windows, :, place : place + frames], shift, 1)
            moved[rows, s * frames : (s + 1) * frames] = jnp.where(inside, window, 0.0).astype(
                jnp.bfloat16
            )

    def multiply(rows):
        return jnp.dot(rows, turned[...], preferred_element_type=jnp.float32) * scale

    def turn(group, now, later):
        slot = lax.rem(group, SLOTS)

        @pl.when(group >= SLOTS)
        def _():
            send(group - SLOTS).wait()

        held[slot] = multiply(now[...]).reshape(held.shape[1:])
        for inner in range(LAG_GROUP):
            fill(later, group + 1, inner)
        send(group).start()

    for inner in range(LAG_GROUP):
        fill(even, 0, inner)
        held[0, inner] = multiply(even[inner * sources : (inner + 1) * sources, :])
        pltpu.make_async_copy(held.at[0, inner], out_ref.at[inner], sems.at[0]).start()
    for inner in range(LAG_GROUP):
        fill(odd, 1, inner)

    def step(index, carry):
        turn(2 * index + 1, odd, even)
        turn(2 * index + 2, even, odd)
        return carry

    lax.fori_loop(0, groups // 2, step, 0)
    for group in range(groups - SLOTS, groups):
        send(group).wait()


def body(rows, cols, record, taps, plan, quality):
    slots, chans, length = record.shape
    width = SUB * (length // STRIDE)
    hbm = pl.BlockSpec(memory_space=pltpu.HBM)
    vmem = pl.BlockSpec(memory_space=pltpu.VMEM)
    anywhere = pl.BlockSpec(memory_space=pl.ANY)
    operands = (plan, taps.reshape(1, TAPS), quality.reshape(1, chans), record)
    sources = cols * chans
    receivers = 2 * sources
    bits = cols.bit_length() - 1
    source, turned = pl.pallas_call(
        functools.partial(whiten_and_send, rows, cols),
        out_shape=(
            jax.ShapeDtypeStruct((CHUNKS, cols, chans, width // CHUNKS), jnp.bfloat16),
            jax.ShapeDtypeStruct((width, receivers), jnp.bfloat16),
        ),
        in_specs=[hbm] * 4,
        out_specs=(vmem, vmem),
        scratch_shapes=[
            pltpu.VMEM((CHUNKS, 2 * cols, chans, width // CHUNKS), jnp.bfloat16),
            pltpu.VMEM((slots, chans, length), jnp.bfloat16),
            pltpu.VMEM((PARTS * (length // STRIDE), length), jnp.bfloat16),
            pltpu.SMEM(plan.shape, jnp.int32),
            pltpu.VMEM((1, TAPS), jnp.float32),
            pltpu.VMEM((1, chans), jnp.int32),
            pltpu.SemaphoreType.DMA((slots + 3,)),
            pltpu.SemaphoreType.DMA((CHUNKS, cols)),
            pltpu.SemaphoreType.DMA((CHUNKS, cols)),
            pltpu.SemaphoreType.DMA((CHUNKS, 2 * cols)),
            pltpu.SemaphoreType.DMA((CHUNKS, cols)),
            pltpu.SemaphoreType.DMA((CHUNKS, cols, bits, 2)),
            pltpu.SemaphoreType.DMA((CHUNKS, cols)),
        ],
        compiler_params=pltpu.CompilerParams(
            collective_id=0, has_side_effects=True, vmem_limit_bytes=32 * 2**20
        ),
        name="whiten_and_send",
    )(*(pltpu.with_memory_space_constraint(held, pltpu.HBM) for held in operands))
    return pl.pallas_call(
        functools.partial(correlate, 1.0 / math.sqrt(width)),
        out_shape=jax.ShapeDtypeStruct((LAGS, sources, receivers), jnp.float32),
        in_specs=[vmem, vmem],
        out_specs=anywhere,
        scratch_shapes=[
            pltpu.VMEM((LAG_GROUP * sources, width), jnp.bfloat16),
            pltpu.VMEM((LAG_GROUP * sources, width), jnp.bfloat16),
            pltpu.VMEM((SLOTS, LAG_GROUP, sources, receivers), jnp.float32),
            pltpu.SemaphoreType.DMA((SLOTS,)),
        ],
        compiler_params=pltpu.CompilerParams(vmem_limit_bytes=32 * 2**20),
        cost_estimate=pl.CostEstimate(
            flops=2 * LAGS * sources * receivers * width,
            bytes_accessed=4 * LAGS * sources * receivers,
            transcendentals=0,
        ),
        name="correlate",
    )(source.reshape(CHUNKS, sources, width // CHUNKS), turned)


def solution(mesh):
    rows, cols = mesh.shape["row"], mesh.shape["col"]
    in_specs = (P(None, ("row", "col"), None), P(), P(), P(("row", "col")))
    out_specs = P(None, "row", "col")
    return jax.shard_map(
        functools.partial(body, rows, cols),
        mesh=mesh,
        in_specs=in_specs,
        out_specs=out_specs,
        check_vma=False,
    )
```

profile of v0, /device:TPU:25, one launch (start us, length us, event | category | flops | bytes accessed | tf_op | source)
XLA Modules:
  0.0 29.7 jit_solution(2166795807271517898)
XLA Ops:
  0.0 18.6 %whiten_and_send.1 = (bf16[2,4,64,256]{3,2,1,0:T(8,128)(2,1)S(1)}, bf16[512,512]{1,0:T(8,128)(2,1)S(1)}) custom-call(s32[6]{0:T(128)} %plan_hbm.1, f32[1,200]{1,0:T(1,128)} %bitcast.4, s32[1,64]{1,0:T(1,128)} %bitcast.5, bf16[6,64,2560]{2,1,0:T(8,128)(2,1)} %record_ref.1), custom_call_target="tpu_custom_call" | custom-call | tf_op jit(solution)/shard_map/whiten_and_send/pallas_call | solution.py:334
  18.6 11.1 %correlate.1 = f32[51,256,512]{2,1,0:T(8,128)} custom-call(bf16[2,256,256]{2,1,0:T(8,128)(2,1)S(1)} %bitcast.3, bf16[512,512]{1,0:T(8,128)(2,1)S(1)} %get-tuple-element.8.turned), custom_call_target="tpu_custom_call" | custom-call | flops 6845104128 | bytes 26738688 | tf_op jit(solution)/shard_map/correlate/pallas_call | solution.py:362
where the time goes:
time: 29.9 us; the launch traced here: 29.7 us
  Pallas kernels  29.7 us (99%)
    pallas_call x1, Pallas kernels, body(): pl.pallas_call(functools.partial(whiten_and_send, rows, cols), out_shape=...  18.6 us
    pallas_call x1, Pallas kernels, body(): pl.pallas_call(functools.partial(correlate, 1.0 / math.sqrt(width)), out_...  11.1 us

commit v1 on v0

--- a/solution.py
+++ b/solution.py
@@ -20,12 +20,10 @@
 BAND_WIDTH = 896
 PARTS = 3
 LAG_GROUP = 3
-SLOTS = 3
+SLOTS = 4
 CHUNKS = 2
 
 MESH = pl.DeviceIdType.MESH
-NT = (((1,), (1,)), ((), ()))
-
 
 def split_parts(values, count):
     parts = []
@@ -99,38 +97,53 @@
         greet(other_core(across(k)), c)
     greet(twin, c)
 
-    table[...] = jnp.zeros_like(table)
     loads[0].wait()
     band = filter_band(tap_ref[...])
+    blocks = frames // BAND_FRAMES
+    band = jnp.concatenate([band] * blocks, axis=0).T
+    lanes = lax.broadcasted_iota(jnp.int32, (BAND_STEP, frames), 1)
+    reach = BAND_WIDTH - BAND_STEP
     for number, part in enumerate(split_parts(band, PARTS)):
-        for block in range(frames // BAND_FRAMES):
-            start = block * BAND_STEP
-            width = min(BAND_WIDTH, length - start)
-            first = number * frames + block * BAND_FRAMES
-            table[first : first + BAND_FRAMES, start : start + width] = part[:, :width]
+        part = part.astype(jnp.float32)
+        for block in range(blocks):
+            first = block * BAND_FRAMES
+            here = jnp.logical_and(lanes >= first, lanes < first + BAND_FRAMES)
+            rows = jnp.where(here, part[:BAND_STEP], 0.0)
+            if block > 0:
+                before = jnp.logical_and(lanes >= first - BAND_FRAMES, lanes < first)
+                head = rows[:reach] + jnp.where(before[:reach], part[BAND_STEP:], 0.0)
+                rows = jnp.concatenate([head, rows[reach:]], axis=0)
+            table[
+                block * BAND_STEP : (block + 1) * BAND_STEP,
+                number * frames : (number + 1) * frames,
+            ] = rows.astype(jnp.bfloat16)
 
     for load in loads[1:]:
         load.wait()
     picked = jnp.concatenate([raw[plan_ref[s]] for s in range(SUB)], axis=0)
-    summed = lax.dot_general(table[...], picked, NT, preferred_element_type=jnp.float32)
-    decimated = summed[:frames]
+    summed = jnp.dot(picked, table[...], preferred_element_type=jnp.float32)
+    decimated = summed[:, :frames]
     for number in range(1, PARTS):
-        decimated = decimated + summed[number * frames : (number + 1) * frames]
+        decimated = decimated + summed[:, number * frames : (number + 1) * frames]
 
     near = lax.broadcasted_iota(jnp.int32, (frames, frames), 0)
     near = jnp.abs(near - lax.broadcasted_iota(jnp.int32, (frames, frames), 1)) <= HALFWIN
     near = near.astype(jnp.float32).astype(jnp.bfloat16)
     windows = SUB // CHUNKS
-    usable = jnp.concatenate([quality_ref[...].astype(jnp.float32)] * windows, axis=1)
+    square = lax.broadcasted_iota(jnp.int32, (chans, chans), 0) == lax.broadcasted_iota(
+        jnp.int32, (chans, chans), 1
+    )
+    usable = jnp.broadcast_to(quality_ref[...].astype(jnp.float32), (chans, chans))
+    usable = jnp.sum(jnp.where(square, usable, 0.0), axis=1, keepdims=True)
 
     def whiten(chunk):
-        part = decimated[:, chunk * windows * chans : (chunk + 1) * windows * chans]
+        part = decimated[chunk * windows * chans : (chunk + 1) * windows * chans]
         envelope = jnp.zeros_like(part)
         for piece in split_parts(jnp.abs(part), PARTS):
-            envelope = envelope + jnp.dot(near, piece, preferred_element_type=jnp.float32)
-        scaled = (part / (envelope / (2 * HALFWIN + 1) + 1e-05) * usable).T
+            envelope = envelope + jnp.dot(piece, near, preferred_element_type=jnp.float32)
+        scaled = part / (envelope / (2 * HALFWIN + 1) + 1e-05)
         for s in range(windows):
-            window = scaled[s * chans : (s + 1) * chans]
+            window = scaled[s * chans : (s + 1) * chans] * usable
             source_ref[chunk, c, :, s * frames : (s + 1) * frames] = window.astype(jnp.bfloat16)
 
     def remote(src, dst, send_sem, recv_sem, row, col):
@@ -276,6 +289,12 @@
             held.at[slot], out_ref.at[pl.ds(group * LAG_GROUP, LAG_GROUP)], sems.at[slot]
         )
 
+    def send_lag(group, inner):
+        slot = lax.rem(group, SLOTS)
+        pltpu.make_async_copy(
+            held.at[slot, inner], out_ref.at[group * LAG_GROUP + inner], sems.at[slot]
+        ).start(priority=inner % 2)
+
     def fill(moved, group, inner):
         lag = group * LAG_GROUP + inner - MAXLAG
         from_place = lane - lag
@@ -302,12 +321,13 @@
         held[slot] = multiply(now[...]).reshape(held.shape[1:])
         for inner in range(LAG_GROUP):
             fill(later, group + 1, inner)
-        send(group).start()
+        for inner in range(LAG_GROUP):
+            send_lag(group, inner)
 
     for inner in range(LAG_GROUP):
         fill(even, 0, inner)
         held[0, inner] = multiply(even[inner * sources : (inner + 1) * sources, :])
-        pltpu.make_async_copy(held.at[0, inner], out_ref.at[inner], sems.at[0]).start()
+        send_lag(0, inner)
     for inner in range(LAG_GROUP):
         fill(odd, 1, inner)
 
@@ -342,7 +362,7 @@
         scratch_shapes=[
             pltpu.VMEM((CHUNKS, 2 * cols, chans, width // CHUNKS), jnp.bfloat16),
             pltpu.VMEM((slots, chans, length), jnp.bfloat16),
-            pltpu.VMEM((PARTS * (length // STRIDE), length), jnp.bfloat16),
+            pltpu.VMEM((length, PARTS * (length // STRIDE)), jnp.bfloat16),
             pltpu.SMEM(plan.shape, jnp.int32),
             pltpu.VMEM((1, TAPS), jnp.float32),
             pltpu.VMEM((1, chans), jnp.int32),

time: 29.9 us -> 29.3 us (0.980)
  Pallas kernels: 29.7 us -> 29.1 us
    pallas_call x1, Pallas kernels: 18.6 us -> 18.1 us  [body(): pl.pallas_call(functools.partial(whiten_and_send, rows, cols), out_shape=...]
where the time goes in v1:
time: 29.3 us; the launch traced here: 29.1 us
  Pallas kernels  29.1 us (99%)
    pallas_call x1, Pallas kernels, body(): pl.pallas_call(functools.partial(whiten_and_send, rows, cols), out_shape=...  18.1 us
    pallas_call x1, Pallas kernels, body(): pl.pallas_call(functools.partial(correlate, 1.0 / math.sqrt(width)), out_...  11 us

profile of v1, /device:TPU:25, one launch (start us, length us, event | category | flops | bytes accessed | tf_op | source)
XLA Modules:
  0.0 29.1 jit_solution(58357288250950835)
XLA Ops:
  0.0 18.1 %whiten_and_send.1 = (bf16[2,4,64,256]{3,2,1,0:T(8,128)(2,1)S(1)}, bf16[512,512]{1,0:T(8,128)(2,1)S(1)}) custom-call(s32[6]{0:T(128)} %plan_hbm.1, f32[1,200]{1,0:T(1,128)} %bitcast.4, s32[1,64]{1,0:T(1,128)} %bitcast.5, bf16[6,64,2560]{2,1,0:T(8,128)(2,1)} %record_ref.1), custom_call_target="tpu_custom_call" | custom-call | tf_op jit(solution)/shard_map/whiten_and_send/pallas_call | solution.py:354
  18.1 11.0 %correlate.1 = f32[51,256,512]{2,1,0:T(8,128)} custom-call(bf16[2,256,256]{2,1,0:T(8,128)(2,1)S(1)} %bitcast.3, bf16[512,512]{1,0:T(8,128)(2,1)S(1)} %get-tuple-element.8.turned), custom_call_target="tpu_custom_call" | custom-call | flops 6845104128 | bytes 26738688 | tf_op jit(solution)/shard_map/correlate/pallas_call | solution.py:382

commit v2 on v1

--- a/solution.py
+++ b/solution.py
@@ -21,7 +21,7 @@
 PARTS = 3
 LAG_GROUP = 3
 SLOTS = 4
-CHUNKS = 2
+CHUNKS = 4
 
 MESH = pl.DeviceIdType.MESH
 

time: 29.3 us -> 29.3 us (level)
  no operation moved by 1% of the time
where the time goes in v2:
time: 29.3 us; the launch traced here: 29.1 us
  Pallas kernels  29.1 us (99%)
    pallas_call x1, Pallas kernels, body(): pl.pallas_call(functools.partial(whiten_and_send, rows, cols), out_shape=...  18.1 us
    pallas_call x1, Pallas kernels, body(): pl.pallas_call(functools.partial(correlate, 1.0 / math.sqrt(width)), out_...  11 us

profile of v2, /device:TPU:25, one launch (start us, length us, event | category | flops | bytes accessed | tf_op | source)
XLA Modules:
  0.0 29.1 jit_solution(4890725687453780346)
XLA Ops:
  0.0 18.1 %whiten_and_send.1 = (bf16[4,4,64,128]{3,2,1,0:T(8,128)(2,1)S(1)}, bf16[512,512]{1,0:T(8,128)(2,1)S(1)}) custom-call(s32[6]{0:T(128)} %plan_hbm.1, f32[1,200]{1,0:T(1,128)} %bitcast.4, s32[1,64]{1,0:T(1,128)} %bitcast.5, bf16[6,64,2560]{2,1,0:T(8,128)(2,1)} %record_ref.1), custom_call_target="tpu_custom_call" | custom-call | tf_op jit(solution)/shard_map/whiten_and_send/pallas_call | solution.py:354
  18.1 11.0 %correlate.1 = f32[51,256,512]{2,1,0:T(8,128)} custom-call(bf16[4,256,128]{2,1,0:T(8,128)(2,1)S(1)} %bitcast.3, bf16[512,512]{1,0:T(8,128)(2,1)S(1)} %get-tuple-element.8.turned), custom_call_target="tpu_custom_call" | custom-call | flops 6845104128 | bytes 26738688 | tf_op jit(solution)/shard_map/correlate/pallas_call | solution.py:382

commit v3 on v2

--- a/solution.py
+++ b/solution.py
@@ -82,9 +82,6 @@
     def across(k):
         return r + 2 * 2**k * (1 - 2 * bit(pair, k))
 
-    def other_core(row):
-        return row + 1 - 2 * parity
-
     barrier = pltpu.get_barrier_semaphore()
 
     def greet(row, col):
@@ -94,7 +91,6 @@
         greet(r, lax.rem(c + step, cols))
     for k in range(bits):
         greet(across(k), c)
-        greet(other_core(across(k)), c)
     greet(twin, c)
 
     loads[0].wait()
@@ -182,7 +178,7 @@
     for chunk in range(CHUNKS):
         whiten(chunk)
         if chunk == 0:
-            pl.semaphore_wait(barrier, cols - 1 + 2 * bits + 1)
+            pl.semaphore_wait(barrier, cols - 1 + bits + 1)
         other, copy = along(chunk, 0)
         pl.when(other)(copy.start)
     for chunk in range(CHUNKS):
@@ -199,7 +195,6 @@
         return number
 
     differs = [bit(pair, k) != bit(c, k) for k in range(bits)]
-    far = sum(jnp.where(differ, 1, 0) for differ in differs) > 1
 
     def passes_on(step, k):
         ahead = range(k + 1) if step % 2 == 0 else range(k, bits)
@@ -240,13 +235,10 @@
             receiver_arrival(chunk, half + number).wait_recv()
             for k in range(bits):
                 sends = passes_on(step, k)
-                for core, to in enumerate((across(k), other_core(across(k)))):
-                    pl.when(sends)(
-                        hand_on(mine, chunk, number, to, plane_sem.at[chunk, step, k, core]).start
-                    )
-            pl.when(jnp.logical_not(far))(
-                hand_on(mine, chunk, number, twin, twin_sem.at[chunk, step]).start
-            )
+                pl.when(sends)(
+                    hand_on(mine, chunk, number, across(k), plane_sem.at[chunk, step, k, 0]).start
+                )
+            hand_on(mine, chunk, number, twin, twin_sem.at[chunk, step]).start()
         for chunk, step in every:
             if step > 0:
                 source_arrival(chunk, lax.rem(c + step, cols)).wait_recv()
@@ -268,12 +260,7 @@
             pl.when(jnp.logical_or(on_diagonal, sends))(
                 hand_on(block, chunk, step, across(k), plane_sem.at[chunk, step, k, 0]).wait_send
             )
-            pl.when(jnp.logical_and(jnp.logical_not(on_diagonal), sends))(
-                hand_on(block, chunk, step, across(k), plane_sem.at[chunk, step, k, 1]).wait_send
-            )
-        pl.when(jnp.logical_not(far))(
-            hand_on(block, chunk, step, twin, twin_sem.at[chunk, step]).wait_send
-        )
+        hand_on(block, chunk, step, twin, twin_sem.at[chunk, step]).wait_send()
 
 
 def correlate(scale, source_ref, turned, out_ref, even, odd, held, sems):
@@ -371,7 +358,7 @@
             pltpu.SemaphoreType.DMA((CHUNKS, cols)),
             pltpu.SemaphoreType.DMA((CHUNKS, 2 * cols)),
             pltpu.SemaphoreType.DMA((CHUNKS, cols)),
-            pltpu.SemaphoreType.DMA((CHUNKS, cols, bits, 2)),
+            pltpu.SemaphoreType.DMA((CHUNKS, cols, bits, 1)),
             pltpu.SemaphoreType.DMA((CHUNKS, cols)),
         ],
         compiler_params=pltpu.CompilerParams(

time: 29.3 us -> 30 us (1.024)
  Pallas kernels: 29.1 us -> 29.8 us
    pallas_call x1, Pallas kernels: 18.1 us -> 18.8 us  [body(): pl.pallas_call(functools.partial(whiten_and_send, rows, cols), out_shape=...]
where the time goes in v3:
time: 30 us; the launch traced here: 29.8 us
  Pallas kernels  29.8 us (99%)
    pallas_call x1, Pallas kernels, body(): pl.pallas_call(functools.partial(whiten_and_send, rows, cols), out_shape=...  18.8 us
    pallas_call x1, Pallas kernels, body(): pl.pallas_call(functools.partial(correlate, 1.0 / math.sqrt(width)), out_...  11 us

profile of v3, /device:TPU:25, one launch (start us, length us, event | category | flops | bytes accessed | tf_op | source)
XLA Modules:
  0.0 29.8 jit_solution(14393697133449094408)
XLA Ops:
  0.0 18.8 %whiten_and_send.1 = (bf16[4,4,64,128]{3,2,1,0:T(8,128)(2,1)S(1)}, bf16[512,512]{1,0:T(8,128)(2,1)S(1)}) custom-call(s32[6]{0:T(128)} %plan_hbm.1, f32[1,200]{1,0:T(1,128)} %bitcast.4, s32[1,64]{1,0:T(1,128)} %bitcast.5, bf16[6,64,2560]{2,1,0:T(8,128)(2,1)} %record_ref.1), custom_call_target="tpu_custom_call" | custom-call | tf_op jit(solution)/shard_map/whiten_and_send/pallas_call | solution.py:341
  18.8 11.0 %correlate.1 = f32[51,256,512]{2,1,0:T(8,128)} custom-call(bf16[4,256,128]{2,1,0:T(8,128)(2,1)S(1)} %bitcast.3, bf16[512,512]{1,0:T(8,128)(2,1)S(1)} %get-tuple-element.8.turned), custom_call_target="tpu_custom_call" | custom-call | flops 6845104128 | bytes 26738688 | tf_op jit(solution)/shard_map/correlate/pallas_call | solution.py:369
